TPU v7x, 256 devices: a whole 4x4x8 slice. The times are simulated.
256 devices in a mesh: sub: 2 (over core), row: 8 (over y_lo, x), col: 16 (over z, y_hi).
Axes of the slice: x: 4, y: 4 (y_hi: 2, y_lo: 2; y = y_hi * 2 + y_lo), z: 8, core: 2. Of those that a mesh axis runs over, the one named last changes fastest.
Arguments:
- initial: float32 [12, 16, 256, 4096], P(None, ('sub', 'row'), None, 'col'), may hold values from -1 to 6
- pattern: int32 [12, 16, 16], P(None, ('sub', 'row'), 'col'), may hold values from 0 to 1, as said below
- rmap: int32 [2, 8, 16], replicated, may hold values from 0 to 191, as said below
- child_update: float32 [2, 8, 16, 256, 4096], P('sub', 'row', None, None, 'col'), may hold values from -0.5 to 0.5
Outputs:
- factored: float32 [12, 16, 256, 4096], P(None, ('sub', 'row'), None, 'col')
Inputs may be any that keep to these rules, and one draw needn't show every extreme that they name: Within one child the 128 entries are distinct tile rows; in each block rmap[c, r, :] exactly two remainders modulo 16 appear 2 times, two never, the others once. pattern[p, p] = 1 for p < 16.
All inputs are finite; a program needn't handle non-finite values.
Results may differ from a plain program's by a relative error of at most 0.0001.
Values sent between devices are 32-bit elements; how exact they have to be, the bound alone decides.
A program may use at most 128 MiB of HBM per device.

v0:
```python
import jax
import jax.numpy as jnp
from jax import lax
from jax.sharding import PartitionSpec as P

CAP = 2


def spread(block, axis, holder):
    block = jnp.where(lax.axis_index(axis) == holder, block, jnp.zeros_like(block))
    return lax.psum(block, axis)


def slot_ranks(tile_map, owners):
    target = tile_map % owners
    index = jnp.arange(target.shape[0])
    earlier = (target[None, :] == target[:, None]) & (index[None, :] < index[:, None])
    return (target, jnp.sum(earlier.astype(jnp.int32), axis=1))


def right_solve(factor, stacked):
    tile = factor.shape[0]
    flat = lax.linalg.triangular_solve(
        factor, stacked.reshape(-1, tile), left_side=False, lower=True, transpose_a=True
    )
    return flat.reshape(stacked.shape)


def per_device(initial, pattern, rmap, child_update):
    owners = lax.axis_size("sub") * lax.axis_size("row")
    frows = initial.shape[0]
    owner_me = lax.axis_index(("sub", "row"))
    child = lax.axis_index("sub")
    proc_row = lax.axis_index("row")
    column_me = lax.axis_index("col")
    slot_ids = jnp.arange(CAP)
    owner_ids = jnp.arange(owners)
    own_map = rmap[child, proc_row]
    target, ranks = slot_ranks(own_map, owners)
    select = (
        (target[None, None, :] == owner_ids[:, None, None])
        & (ranks[None, None, :] == slot_ids[None, :, None])
    ).astype(jnp.float32)
    outgoing = jnp.einsum(
        "dsk,kab->dsab", select, child_update[0, 0], precision=lax.Precision.HIGHEST
    )
    incoming = lax.all_to_all(outgoing, ("sub", "row"), split_axis=0, concat_axis=0, tiled=True)
    all_maps = rmap.reshape(owners, owners)
    all_target, all_ranks = jax.vmap(lambda one: slot_ranks(one, owners))(all_maps)
    local_row = all_maps // owners
    placing = (
        (all_target == owner_me)[None, :, None, :]
        & (all_ranks[None, :, None, :] == slot_ids[None, None, :, None])
        & (local_row[None, :, None, :] == jnp.arange(frows)[:, None, None, None])
    )
    placing = jnp.sum(placing.astype(jnp.float32), axis=3)
    front = initial[:, 0] * pattern[:, 0, :, None].astype(jnp.float32)
    front = front + jnp.einsum("msj,sjab->mab", placing, incoming, precision=lax.Precision.HIGHEST)
    tile_row = jnp.arange(frows) * owners + owner_me
    for step in range(2):
        column = spread(front, "col", step)
        diag = spread(column[step // owners], ("sub", "row"), step % owners)
        factor = jnp.linalg.cholesky(diag)
        solved = right_solve(factor, column)
        panel = jnp.where(
            (tile_row == step)[:, None, None],
            factor[None],
            jnp.where((tile_row > step)[:, None, None], solved, jnp.zeros_like(solved)),
        )
        own_tile = lax.dynamic_index_in_dim(panel, column_me // owners, 0, keepdims=False)
        row_tile = spread(own_tile, ("sub", "row"), column_me % owners)
        update = jnp.einsum("mab,cb->mac", panel, row_tile, precision=lax.Precision.HIGHEST)
        lower = (column_me > step) & (tile_row > step)[:, None, None]
        front = jnp.where(column_me == step, panel, jnp.where(lower, front - update, front))
    return front[:, None]


def solution(mesh):
    return jax.shard_map(
        per_device,
        mesh=mesh,
        in_specs=(
            P(None, ("sub", "row"), None, "col"),
            P(None, ("sub", "row"), "col"),
            P(),
            P("sub", "row", None, None, "col"),
        ),
        out_specs=P(None, ("sub", "row"), None, "col"),
        check_vma=False,
    )
```

profile of v0, /device:TPU:6, one launch (start us, length us, event | category | flops | bytes accessed | tf_op | source)
XLA Modules:
  0.0 1269.4 jit_solution(1868014286174128155)
XLA Ops:
  8.1 7.7 fusion.2
  15.9 9.7 copy.61
  25.6 6.7 all-to-all-start
  35.4 107.6 %all-to-all-done = f32[16,2,256,256]{3,1,2,0:T(2,128)} async-done(((f32[16,2,256,256]{3,1,2,0:T(2,128)}), f32[16,2,256,256]{3,1,2,0:T(2,128)}, u32[]{:S(2)}, u32[]{:S(2)}) %all-to-all-start) | async-done | bytes 8388640 | tf_op jit(solution)/shard_map/all_to_all | solution.py:47
  143.1 13.4 %fusion.9 = f32[12,256,256]{2,0,1:T(8,128)} fusion(f32[16,2,256,256]{3,1,2,0:T(2,128)} %all-to-all-done, f32[12,16,2]{1,2,0:T(2,128)S(1)} %convert_reduce_fusion), kind=kOutput, calls=%fused_computation.22 | convolution fusion | flops 301989888 | bytes 11535872 | tf_op jit(solution)/shard_map/msj,sjab->mab/dot_general | solution.py:58
  156.5 4.9 copy.64
  161.3 4.1 broadcast_select_fusion.1
  165.5 181.0 %all-reduce.8.cloned.1.call-done = f32[12,256,256]{1,2,0:T(8,128)} async-done(((f32[12,256,256]{1,2,0:T(8,128)}), f32[12,256,256]{1,2,0:T(8,128)}) %all-reduce.8.cloned.1.call-update) | async-done | bytes 3145744 | tf_op jit(solution)/shard_map/psum | solution.py:11
  352.5 128.7 %all-reduce.10.cloned.1.call-done = f32[256,256]{0,1:T(8,128)} async-done(((f32[256,256]{0,1:T(8,128)}), f32[256,256]{0,1:T(8,128)}) %all-reduce.10.cloned.1.call-update) | async-done | bytes 262160 | tf_op jit(solution)/shard_map/psum | solution.py:11
  484.0 11.7 cholesky.130
  495.8 9.8 custom-call.13
  507.8 11.7 cholesky.147
  524.5 4.0 while.4
  529.2 20.7 %custom-call.14 = f32[2,128,128]{1,2,0:T(8,128)S(1)} custom-call(f32[2,128,128]{2,1,0:T(8,128)} %copy-done.8), custom_call_target="InvertDiagBlocksLowerTriangular" | custom-call | tf_op jit(solution)/shard_map/triangular_solve/custom-call.0 | solution.py:23
  572.2 136.1 %all-reduce.12.cloned.1.call-done = f32[256,256]{0,1:T(8,128)} async-done(((f32[256,256]{0,1:T(8,128)}), f32[256,256]{0,1:T(8,128)}) %all-reduce.12.cloned.1.call-update) | async-done | bytes 262160 | tf_op jit(solution)/shard_map/psum | solution.py:11
  708.3 10.2 broadcast_select_fusion
  718.6 181.2 %all-reduce.14.cloned.1.call-done = f32[12,256,256]{1,2,0:T(8,128)} async-done(((f32[12,256,256]{1,2,0:T(8,128)}), f32[12,256,256]{1,2,0:T(8,128)}) %all-reduce.14.cloned.1.call-update) | async-done | bytes 3145744 | tf_op jit(solution)/shard_map/psum | solution.py:11
  904.4 129.5 %all-reduce.16.cloned.1.call-done = f32[256,256]{0,1:T(8,128)} async-done(((f32[256,256]{0,1:T(8,128)}), f32[256,256]{0,1:T(8,128)}) %all-reduce.16.cloned.1.call-update) | async-done | bytes 262160 | tf_op jit(solution)/shard_map/psum | solution.py:11
  1036.6 11.7 cholesky.164
  1048.4 9.8 custom-call.15
  1060.4 11.7 cholesky.181
  1080.7 20.6 %custom-call.16 = f32[2,128,128]{1,2,0:T(8,128)S(1)} custom-call(f32[2,128,128]{2,1,0:T(8,128)} %copy-done.7), custom_call_target="InvertDiagBlocksLowerTriangular" | custom-call | tf_op jit(solution)/shard_map/triangular_solve/custom-call.0 | solution.py:23
  1116.6 136.2 %all-reduce.18.cloned.1.call-done = f32[256,256]{0,1:T(8,128)} async-done(((f32[256,256]{0,1:T(8,128)}), f32[256,256]{0,1:T(8,128)}) %all-reduce.18.cloned.1.call-update) | async-done | bytes 262160 | tf_op jit(solution)/shard_map/psum | solution.py:11
  1252.8 6.0 fusion.7
  (113 shorter events, 85.7 us)
Async XLA Ops:
  25.6 117.5 %all-to-all-start = ((f32[16,2,256,256]{3,1,2,0:T(2,128)}), f32[16,2,256,256]{3,1,2,0:T(2,128)}, u32[]{:S(2)}, u32[]{:S(2)}) async-start(f32[16,2,256,256]{3,1,2,0:T(2,128)} %copy.61), calls=%async_computation | async-start | bytes 16777216 | tf_op jit(solution)/shard_map/all_to_all | solution.py:47
  32.3 314.3 %all-reduce.8.cloned.1.call-start = ((), (), s32[]{:S(2)}) async-start(), calls=%async_computation.1 | async-start | bytes 6291456 | tf_op jit(solution)/shard_map/psum | solution.py:11
  32.3 2.4 copy-start.9
  32.3 3.1 copy-start.10
  165.4 315.8 %all-reduce.10.cloned.1.call-start = ((), (), s32[]{:S(2)}) async-start(), calls=%async_computation.2 | async-start | bytes 524288 | tf_op jit(solution)/shard_map/psum | solution.py:11
  348.2 360.1 %all-reduce.12.cloned.1.call-start = ((), (), s32[]{:S(2)}) async-start(), calls=%async_computation.3 | async-start | bytes 524288 | tf_op jit(solution)/shard_map/psum | solution.py:11
  483.3 0.7 copy-start.5
  519.5 2.6 copy-start.2
  528.5 0.6 copy-start.8
  549.8 3.1 copy-start.1
  569.7 1.7 copy-start
  572.2 327.7 %all-reduce.14.cloned.1.call-start = ((), (), s32[]{:S(2)}) async-start(), calls=%async_computation.4 | async-start | bytes 6291456 | tf_op jit(solution)/shard_map/psum | solution.py:11
  718.5 315.3 %all-reduce.16.cloned.1.call-start = ((), (), s32[]{:S(2)}) async-start(), calls=%async_computation.5 | async-start | bytes 524288 | tf_op jit(solution)/shard_map/psum | solution.py:11
  901.5 351.3 %all-reduce.18.cloned.1.call-start = ((), (), s32[]{:S(2)}) async-start(), calls=%async_computation.6 | async-start | bytes 524288 | tf_op jit(solution)/shard_map/psum | solution.py:11
  1035.9 0.7 copy-start.6
  1072.1 2.4 copy-start.3
  1080.1 0.7 copy-start.7
  1109.7 3.6 copy-start.4
Sparse Core Ops, SparseCore 0:
  165.5 180.9 all-reduce.7
  349.1 132.0 all-reduce.9
  572.3 135.9 all-reduce.11
  718.7 181.0 all-reduce.13
  902.3 131.5 all-reduce.15
  1116.7 136.0 all-reduce.17
where the time goes:
time: 1280 us; the launch traced here: 1270 us
  waiting for transfers between devices  1000 us (78%)
  other arithmetic  134 us (10%)
  local copies, waits for them, and re-layouts  55.7 us (4%)
  matrix products  54.8 us (4%)
  between operations  16.6 us (1%)
    psum x6, waiting for transfers between devices, spread(): return lax.psum(block, axis)  893 us
    all_to_all x1, waiting for transfers between devices, per_device(): lax.all_to_all(outgoing, ('sub', 'row'), split_axis=0, concat_axis=0, til...  108 us
    another operation x14, other arithmetic, per_device(): factor = jnp.linalg.cholesky(diag)  69.2 us
    another operation x7, other arithmetic, right_solve(): lax.linalg.triangular_solve(factor, stacked.reshape(-1, tile), left_side=...  47.5 us
  transfers between devices with their start and end apart: 7, of which 7 were waited for; matrix products, arithmetic and copies ran while one was open for 1% of the time, Pallas kernels for 0%

commit v1 on v0

--- a/solution.py
+++ b/solution.py
@@ -8,7 +8,7 @@
 
 def spread(block, axis, holder):
     block = jnp.where(lax.axis_index(axis) == holder, block, jnp.zeros_like(block))
-    return lax.psum(block, axis)
+    return jnp.sum(lax.all_gather(block, axis), axis=0)
 
 
 def slot_ranks(tile_map, owners):

time: 1280 us -> 1810 us (1.41)
  waiting for transfers between devices: 1000 us -> 1470 us
  other arithmetic: 134 us -> 200 us
    all_gather x0 -> x6, waiting for transfers between devices: none -> 1360 us  [spread(): return jnp.sum(lax.all_gather(block, axis), axis=0)]
    psum x6 -> x0, waiting for transfers between devices: 893 us -> none  [spread(): return lax.psum(block, axis)]
    reduce_sum x0 -> x6, other arithmetic: none -> 48.8 us  [spread(): return jnp.sum(lax.all_gather(block, axis), axis=0)]
  transfers between devices with their start and end apart: 7 -> 7, of which waited for: 7 -> 7; matrix products, arithmetic and copies ran while one was open for 1% -> 0% of each run, Pallas kernels for 0% -> 0%
where the time goes in v1:
time: 1810 us; the launch traced here: 1800 us
  waiting for transfers between devices  1470 us (81%)
  other arithmetic  200 us (11%)
  matrix products  56.4 us (3%)
  local copies, waits for them, and re-layouts  53.2 us (3%)
    all_gather x6, waiting for transfers between devices, spread(): return jnp.sum(lax.all_gather(block, axis), axis=0)  1360 us
    all_to_all x1, waiting for transfers between devices, per_device(): lax.all_to_all(outgoing, ('sub', 'row'), split_axis=0, concat_axis=0, til...  110 us
    another operation x14, other arithmetic, per_device(): factor = jnp.linalg.cholesky(diag)  71.1 us
    reduce_sum x6, other arithmetic, spread(): return jnp.sum(lax.all_gather(block, axis), axis=0)  48.8 us
    another operation x7, other arithmetic, right_solve(): lax.linalg.triangular_solve(factor, stacked.reshape(-1, tile), left_side=...  48.4 us
  transfers between devices with their start and end apart: 7, of which 7 were waited for; matrix products, arithmetic and copies ran while one was open for 0% of the time, Pallas kernels for 0%

profile of v1, /device:TPU:6, one launch (start us, length us, event | category | flops | bytes accessed | tf_op | source)
XLA Modules:
  0.0 1800.6 jit_solution(16571866450314409746)
XLA Ops:
  8.1 7.7 fusion.5
  15.9 9.7 copy.56
  25.6 7.0 all-to-all-start
  33.4 109.9 %all-to-all-done = f32[16,2,256,256]{3,1,2,0:T(2,128)} async-done(((f32[16,2,256,256]{3,1,2,0:T(2,128)}), f32[16,2,256,256]{3,1,2,0:T(2,128)}, u32[]{:S(2)}, u32[]{:S(2)}) %all-to-all-start) | async-done | bytes 8388640 | tf_op jit(solution)/shard_map/all_to_all | solution.py:47
  143.3 15.8 broadcast_select_fusion.1
  162.7 602.6 %all-gather.17.cloned.1.call-done = f32[192,256,256]{2,1,0:T(8,128)} async-done(((f32[12,256,256]{2,1,0:T(8,128)}), f32[192,256,256]{2,1,0:T(8,128)}) %all-gather.17.cloned.1.call-update) | async-done | bytes 50331664 | tf_op jit(solution)/shard_map/all_gather | solution.py:11
  765.3 17.6 reduce_sum.84
  784.3 35.8 %all-gather.9.cloned.1.call-done = f32[16,256,256]{2,1,0:T(8,128)} async-done(((f32[1,256,256]{2,1,0:T(8,128)}), f32[16,256,256]{2,1,0:T(8,128)}) %all-gather.9.cloned.1.call-update) | async-done | bytes 4194320 | tf_op jit(solution)/shard_map/all_gather | solution.py:11
  825.1 11.7 cholesky.130
  836.9 9.8 custom-call.13
  848.8 11.7 cholesky.147
  871.9 20.5 %custom-call.14 = f32[2,128,128]{1,2,0:T(8,128)S(1)} custom-call(f32[2,128,128]{2,1,0:T(8,128)} %copy-done.11), custom_call_target="InvertDiagBlocksLowerTriangular" | custom-call | tf_op jit(solution)/shard_map/triangular_solve/custom-call.0 | solution.py:23
  908.6 40.1 %all-gather.11.cloned.1.call-done = f32[16,256,256]{2,1,0:T(8,128)} async-done(((f32[1,256,256]{2,1,0:T(8,128)}), f32[16,256,256]{2,1,0:T(8,128)}) %all-gather.11.cloned.1.call-update) | async-done | bytes 4194320 | tf_op jit(solution)/shard_map/all_gather | solution.py:11
  966.1 602.1 %all-gather.19.cloned.1.call-done = f32[192,256,256]{2,1,0:T(8,128)} async-done(((f32[12,256,256]{2,1,0:T(8,128)}), f32[192,256,256]{2,1,0:T(8,128)}) %all-gather.19.cloned.1.call-update) | async-done | bytes 50331664 | tf_op jit(solution)/shard_map/all_gather | solution.py:11
  1568.2 19.3 %reduce_sum.87 = f32[12,256,256]{2,1,0:T(8,128)} reduce(f32[16,12,256,256]{3,2,1,0:T(8,128)} %bitcast.133, f32[]{:T(128)} %constant.149.clone.1), dimensions={0}, to_apply=%region_10.13 | reduce | flops 11796480 | bytes 53477380 | tf_op jit(solution)/shard_map/reduce_sum | solution.py:11
  1590.2 35.3 %all-gather.13.cloned.1.call-done = f32[16,256,256]{2,1,0:T(8,128)} async-done(((f32[1,256,256]{2,1,0:T(8,128)}), f32[16,256,256]{2,1,0:T(8,128)}) %all-gather.13.cloned.1.call-update) | async-done | bytes 4194320 | tf_op jit(solution)/shard_map/all_gather | solution.py:11
  1632.2 11.7 cholesky.164
  1645.2 9.8 custom-call.15
  1657.8 11.7 cholesky.181
  1675.2 7.8 while.5
  1683.7 20.5 %custom-call.16 = f32[2,128,128]{1,2,0:T(8,128)S(1)} custom-call(f32[2,128,128]{2,1,0:T(8,128)} %copy-done.12), custom_call_target="InvertDiagBlocksLowerTriangular" | custom-call | tf_op jit(solution)/shard_map/triangular_solve/custom-call.0 | solution.py:23
  1725.0 40.1 %all-gather.15.cloned.1.call-done = f32[16,256,256]{2,1,0:T(8,128)} async-done(((f32[1,256,256]{2,1,0:T(8,128)}), f32[16,256,256]{2,1,0:T(8,128)}) %all-gather.15.cloned.1.call-update) | async-done | bytes 4194320 | tf_op jit(solution)/shard_map/all_gather | solution.py:11
  1768.3 6.6 fusion.10
  1774.9 15.2 fusion.4
  (132 shorter events, 117.2 us)
Async XLA Ops:
  25.6 7.2 copy-start.13
  25.6 7.9 copy-start.15
  25.6 117.8 %copy-start.6 = (f32[12,1,256,256]{3,2,1,0:T(8,128)S(1)}, f32[12,1,256,256]{3,2,1,0:T(8,128)}, u32[]{:S(2)}) copy-start(f32[12,1,256,256]{3,2,1,0:T(8,128)} %param.7) | copy-start | bytes 9437188
  25.6 117.8 %all-to-all-start = ((f32[16,2,256,256]{3,1,2,0:T(2,128)}), f32[16,2,256,256]{3,1,2,0:T(2,128)}, u32[]{:S(2)}, u32[]{:S(2)}) async-start(f32[16,2,256,256]{3,1,2,0:T(2,128)} %copy.56), calls=%async_computation | async-start | bytes 16777216 | tf_op jit(solution)/shard_map/all_to_all | solution.py:47
  32.5 732.8 %all-gather.17.cloned.1.call-start = ((), (), s32[]{:S(2)}) async-start(), calls=%async_computation.5 | async-start | bytes 53477376 | tf_op jit(solution)/shard_map/all_gather | solution.py:11
  162.7 657.4 %all-gather.9.cloned.1.call-start = ((), (), s32[]{:S(2)}) async-start(), calls=%async_computation.1 | async-start | bytes 4456448 | tf_op jit(solution)/shard_map/all_gather | solution.py:11
  784.0 164.7 %all-gather.11.cloned.1.call-start = ((), (), s32[]{:S(2)}) async-start(), calls=%async_computation.2 | async-start | bytes 4456448 | tf_op jit(solution)/shard_map/all_gather | solution.py:11
  824.4 0.7 copy-start.9
  860.6 2.7 copy-start.8
  871.3 0.6 copy-start.11
  871.9 27.1 %copy-start.16 = (s32[2,2]{1,0:T(2,128)}, s32[2,2]{1,0:T(2,128)S(1)}, u32[]{:S(2)}) copy-start(s32[2,2]{1,0:T(2,128)S(1)} %get-tuple-element.184) | copy-start | bytes 52
  905.5 1.9 copy-start.4
  908.5 659.7 %all-gather.19.cloned.1.call-start = ((), (), s32[]{:S(2)}) async-start(), calls=%async_computation.6 | async-start | bytes 53477376 | tf_op jit(solution)/shard_map/all_gather | solution.py:11
  951.8 6.6 copy-start
  958.4 4.1 copy-start.2
  966.0 659.5 %all-gather.13.cloned.1.call-start = ((), (), s32[]{:S(2)}) async-start(), calls=%async_computation.3 | async-start | bytes 4456448 | tf_op jit(solution)/shard_map/all_gather | solution.py:11
  1589.4 175.7 %all-gather.15.cloned.1.call-start = ((), (), s32[]{:S(2)}) async-start(), calls=%async_computation.4 | async-start | bytes 4456448 | tf_op jit(solution)/shard_map/all_gather | solution.py:11
  1631.5 0.7 copy-start.10
  1683.1 0.7 copy-start.12
  1704.2 3.1 copy-start.5
  1714.4 3.6 copy-start.14
  1722.0 1.9 copy-start.3
  1768.3 6.6 copy-start.1
  1768.3 6.6 copy-start.7
Sparse Core Ops, SparseCore 0:
  162.8 602.5 all-gather.16
  784.1 35.9 all-gather.8
  908.6 39.9 all-gather.10
  966.2 601.9 all-gather.18
  1589.5 35.9 all-gather.12
  1725.1 39.9 all-gather.14
